TPU v7x, 1024 devices: a whole 4x8x16 slice. The times are simulated.
1024 devices in a mesh: dp: 64 (over z, x), expert: 16 (over y, core).
Axes of the slice: x: 4, y: 8, z: 16, core: 2. Of those that a mesh axis runs over, the one named last changes fastest.
Arguments:
- tokens: bfloat16 [8192, 4096], P('dp'), may hold values from -6 to 6
- out_grad: bfloat16 [8192, 4096], P('dp'), may hold values from -6 to 6
- w_in: bfloat16 [16, 6656, 4096], P('expert', 'dp'), may hold values from -0.09375 to 0.09375
- w_out: bfloat16 [16, 6656, 4096], P('expert', 'dp'), may hold values from -0.0546875 to 0.0546875
- gates: float32 [8, 192], P(None, 'dp'), may hold values from 0.1 to 1
- picks: int32 [8, 192], P(None, 'dp'), may hold values from 0 to 127, as said below
- counts: int32 [8, 64], P(None, 'dp'), may hold values from 0 to 3, as said below
Outputs:
- grad_tokens: bfloat16 [8192, 4096], P('dp', 'expert')
- grad_in: bfloat16 [16, 6656, 4096], P('expert', 'dp')
- grad_out: bfloat16 [16, 6656, 4096], P('expert', 'dp')
- grad_gates: float32 [8, 192], P(None, 'dp')
Inputs may be any that keep to these rules, and one draw needn't show every extreme that they name: Within each tile of 3 slots of one expert (slots s * 3 to s * 3 + 2, which belong to shard s) the picks are distinct rows of that shard, padded slots included; a token row may be picked by any number of experts. Only the first counts[e, s] slots of a tile are valid; every expert has at least one full tile.
All inputs are finite; a program needn't handle non-finite values.
Results may differ from a plain program's by a relative error of at most 0.02.
Values may be sent and summed in bfloat16 or wider, within the bound.
A program may use at most 32 MiB of HBM per device.

v0:
```python
import jax
import jax.numpy as jnp
from jax import lax
from jax.sharding import PartitionSpec as P

SPLIT = 2


gelu_coef = 0.7978845608
cubic_coef = 0.044715


def gelu_tanh(value):
    inner = jnp.tanh(gelu_coef * (value + cubic_coef * value * value * value))
    return 0.5 * value * (1.0 + inner)


def gelu_slope(value):
    inner = jnp.tanh(gelu_coef * (value + cubic_coef * value * value * value))
    return 0.5 * (1.0 + inner) + 0.5 * value * (1.0 - inner * inner) * gelu_coef * (
        1.0 + 3.0 * cubic_coef * value * value
    )


def on_device(tokens, out_grad, w_in, w_out, gates, picks, counts):
    owner_index = lax.axis_index("expert")
    expert_id = owner_index // SPLIT
    expert_total = picks.shape[0]
    my_picks = lax.dynamic_index_in_dim(picks, expert_id, 0, keepdims=False)
    my_gates = lax.dynamic_index_in_dim(gates, expert_id, 0, keepdims=False)
    my_count = lax.dynamic_index_in_dim(counts, expert_id, 0, keepdims=False)[0]
    slot_count = my_picks.shape[0]
    slot_ids = jnp.arange(slot_count, dtype=jnp.int32)
    is_valid = slot_ids < my_count
    weight = jnp.where(is_valid, my_gates, jnp.zeros_like(my_gates))
    token_rows = jnp.take(tokens, my_picks, axis=0)
    grad_rows = jnp.take(out_grad, my_picks, axis=0)
    token_all, grad_all, weight_all = (
        lax.all_gather(token_rows, "dp", axis=0, tiled=True),
        lax.all_gather(grad_rows, "dp", axis=0, tiled=True),
        lax.all_gather(weight.astype(jnp.bfloat16), "dp", axis=0, tiled=True).astype(weight.dtype),
    )
    first_proj = w_in[0]
    second_proj = w_out[0]
    contract_last = (((1,), (1,)), ((), ()))
    contract_first = (((0,), (0,)), ((), ()))
    pre_act = lax.dot_general(
        first_proj, token_all, contract_last, preferred_element_type=jnp.float32
    )
    activation = gelu_tanh(pre_act).astype(jnp.bfloat16)
    back_proj = lax.dot_general(
        second_proj, grad_all, contract_last, preferred_element_type=jnp.float32
    )
    d_pre = (back_proj * weight_all[None, :] * gelu_slope(pre_act)).astype(jnp.bfloat16)
    upstream = (grad_all.astype(jnp.float32) * weight_all[:, None]).astype(jnp.bfloat16)
    grad_second = jnp.dot(activation, upstream, preferred_element_type=jnp.float32).astype(
        jnp.bfloat16
    )
    grad_first = jnp.dot(d_pre, token_all, preferred_element_type=jnp.float32).astype(jnp.bfloat16)
    partial_score = jnp.sum(activation.astype(jnp.float32) * back_proj, axis=0)
    expert_rows = jnp.arange(expert_total, dtype=jnp.int32)
    score_table = jnp.where(
        expert_rows[:, None] == expert_id,
        partial_score[None, :],
        jnp.zeros((expert_total, partial_score.shape[0]), jnp.float32),
    )
    score_total = lax.psum(score_table, ("dp", "expert"))
    dp_index = lax.axis_index("dp")
    my_scores = lax.dynamic_slice_in_dim(score_total, dp_index * slot_count, slot_count, 1)
    valid_table = slot_ids[None, :] < counts
    grad_gates = jnp.where(valid_table, my_scores, jnp.zeros_like(my_scores))
    row_match = (jnp.arange(tokens.shape[0], dtype=jnp.int32)[:, None] == my_picks[None, :]).astype(
        jnp.float32
    )
    slot_tile = lax.psum_scatter(
        lax.dot_general(d_pre, first_proj, contract_first, preferred_element_type=jnp.float32),
        "dp",
        scatter_dimension=0,
        tiled=True,
    )
    spread = jnp.dot(row_match, slot_tile, precision=lax.Precision.HIGHEST)
    grad_tokens = lax.psum_scatter(
        spread.astype(jnp.bfloat16), "expert", scatter_dimension=1, tiled=True
    )
    return (grad_tokens, grad_first[None], grad_second[None], grad_gates)


def solution(mesh):
    placed = (
        P("dp", None),
        P("dp", None),
        P("expert", "dp", None),
        P("expert", "dp", None),
        P(None, "dp"),
        P(None, "dp"),
        P(None, "dp"),
    )
    return jax.shard_map(
        on_device,
        mesh=mesh,
        in_specs=placed,
        out_specs=(
            P("dp", "expert"),
            P("expert", "dp", None),
            P("expert", "dp", None),
            P(None, "dp"),
        ),
        check_vma=False,
    )
```

profile of v0, /device:TPU:1, one launch (start us, length us, event | category | flops | bytes accessed | tf_op | source)
XLA Modules:
  0.0 750.1 jit_solution(12235669165169092139)
XLA Ops:
  7.2 0.0 all-gather.7.cloned.1.call-start
  7.2 0.9 dynamic-slice_reduce_fusion.1
  8.2 0.2 copy-done
  8.4 0.6 gather_fusion.1
  9.0 2.0 gather_fusion
  11.0 0.7 select_bitcast_fusion.1
  11.7 0.0 all-gather.7.cloned.1.call-update
  11.7 0.0 all-gather.5.cloned.1.call-start
  11.8 0.7 all-gather.5.cloned.1.call-update
  12.5 0.0 all-reduce.4.cloned.1.call-start
  12.5 1.2 constant_dynamic-slice_fusion
  13.8 0.9 dynamic-slice_reduce_fusion
  14.6 1.4 fusion.18
  16.6 0.7 fusion.16
  17.3 0.2 dynamic-update-slice
  17.5 129.9 %all-reduce = bf16[192]{0:T(256)(128)(2,1)S(1)} all-reduce(bf16[192]{0:T(256)(128)(2,1)S(1)} %dynamic-update-slice), channel_id=1, replica_groups=mesh['dp'=64,'expert'=16] {'dp'}, use_global_device_ids=true, to_apply=%add | all-reduce | flops 192 | bytes 768
  147.4 13.1 %all-gather.7.cloned.1.call-done = bf16[64,3,4096]{2,1,0:T(4,128)(2,1)} async-done(((bf16[1,3,4096]{2,1,0:T(4,128)(2,1)}), bf16[64,3,4096]{2,1,0:T(4,128)(2,1)}) %all-gather.7.cloned.1.call-update) | async-done | bytes 1572880 | tf_op jit(solution)/shard_map/all_gather | solution.py:39
  160.5 3.1 reshape.46
  163.7 1.2 convolution_bitcast_fusion
  164.9 143.1 %all-gather.5.cloned.1.call-done = bf16[64,3,4096]{2,1,0:T(4,128)(2,1)} async-done(((bf16[1,3,4096]{2,1,0:T(4,128)(2,1)}), bf16[64,3,4096]{2,1,0:T(4,128)(2,1)}) %all-gather.5.cloned.1.call-update) | async-done | bytes 1572880 | tf_op jit(solution)/shard_map/all_gather | solution.py:40
  308.1 4.3 reshape.44
  312.3 2.3 multiply_reduce_fusion
  314.7 2.3 fusion.3
  317.0 0.0 reduce-scatter.2.cloned.1.call-start
  317.7 292.7 %all-reduce.4.cloned.1.call-done = f32[192,4096]{1,0:T(8,128)} async-done(((f32[192,4096]{1,0:T(8,128)}), f32[192,4096]{1,0:T(8,128)}) %all-reduce.4.cloned.1.call-update) | async-done | bytes 3145744
  610.3 2.9 convolution_convert_fusion
  613.3 0.1 broadcast_select_fusion
  613.4 126.7 %psum.7 = f32[8,192]{0,1:T(8,128)S(1)} all-reduce(f32[8,192]{0,1:T(8,128)S(1)} %broadcast_select_fusion), channel_id=1, replica_groups=mesh['dp'=64,'expert'=16] {'dp','expert'}, use_global_device_ids=true, to_apply=%region_3.5 | all-reduce | flops 1536 | bytes 12288 | tf_op jit(solution)/shard_map/psum | solution.py:67
  740.1 1.3 fusion
  741.4 0.2 copy-done.1
  741.6 1.4 fusion.1
  743.0 0.6 dynamic-slice_select_fusion
  (17 shorter events, 0.1 us)
Async XLA Ops:
  7.2 1.2 copy-start
  7.2 153.4 %all-gather.7.cloned.1.call-start = ((), (), s32[]{:S(2)}) async-start(), calls=%async_computation.3 | async-start | bytes 2129920 | tf_op jit(solution)/shard_map/all_gather | solution.py:39
  11.7 296.3 %all-gather.5.cloned.1.call-start = ((), (), s32[]{:S(2)}) async-start(), calls=%async_computation.2 | async-start | bytes 2129920 | tf_op jit(solution)/shard_map/all_gather | solution.py:40
  12.5 597.9 %all-reduce.4.cloned.1.call-start = ((), (), s32[]{:S(2)}) async-start(), calls=%async_computation.4 | async-start | bytes 6291456
  147.4 16.3 %copy-start.2 = (bf16[1,104,4096]{2,1,0:T(8,128)(2,1)S(1)}, bf16[1,104,4096]{2,1,0:T(8,128)(2,1)}, u32[]{:S(2)}) copy-start(bf16[1,104,4096]{2,1,0:T(8,128)(2,1)} %param.11) | copy-start | bytes 2555908
  317.0 426.6 %reduce-scatter.2.cloned.1.call-start = ((), (), s32[]{:S(2)}) async-start(), calls=%async_computation.1 | async-start | bytes 1114112 | tf_op jit(solution)/shard_map/reduce_scatter | solution.py:82
  613.3 128.1 %copy-start.3 = (f32[104,192]{0,1:T(8,128)S(1)}, f32[104,192]{0,1:T(8,128)}, u32[]{:S(2)}) copy-start(f32[104,192]{0,1:T(8,128)} %convolution_bitcast_fusion) | copy-start | bytes 239620
  740.1 1.5 copy-start.1
  741.6 1.4 copy-start.4
Sparse Core Ops, SparseCore 0:
  12.7 147.7 all-gather.6
  165.2 142.7 all-gather.4
  317.1 293.1 all-reduce.3
  614.2 67.8 reduce-scatter.1
where the time goes:
time: 751 us; the launch traced here: 750 us
  waiting for transfers between devices  450 us (60%)
  blocking collectives  257 us (34%)
  between operations  15.2 us (2%)
  local copies, waits for them, and re-layouts  15 us (2%)
  matrix products  11.5 us (2%)
    unnamed x5, waiting for transfers between devices  293 us
    all_gather x1, waiting for transfers between devices, on_device(): lax.all_gather(grad_rows, 'dp', axis=0, tiled=True)  143 us
    unnamed x1, blocking collectives  130 us
    psum x1, blocking collectives, on_device(): score_total = lax.psum(score_table, ('dp', 'expert'))  127 us
  transfers between devices with their start and end apart: 4, of which 3 were waited for; matrix products, arithmetic and copies ran while one was open for 2% of the time, Pallas kernels for 0%

commit v1 on v0

v1 whole, which is shorter than its diff:
```python
import jax
import jax.numpy as jnp
from jax import lax
from jax.experimental import pallas as pl
from jax.experimental.pallas import tpu as pltpu
from jax.sharding import PartitionSpec as P

MESH = pl.DeviceIdType.MESH
f32 = jnp.float32
bf16 = jnp.bfloat16

gelu_coef = 0.7978845608
cubic_coef = 0.044715

NX, NY, NZ = 4, 8, 16
SLOTS = 3
D = 4096
HID = 104


def device(z, x, y, core):
    return (z * NX + x, y * 2 + core)


def iota(shape, dim):
    return lax.broadcasted_iota(jnp.int32, shape, dim)


def kernel(
    tok_hbm, og_hbm, win_hbm, wout_hbm, gates, picks, counts,
    gtok_out, gin_hbm, gout_hbm, ggate_out,
    src, win, wout, rows_buf, full_tok, full_og, wt_own, wt_in,
    part_own, part_send, part_in, fold, red1, sum1, red2, sum2, red3, total,
    score_own, score_in, msg, msg_in, gin, gout,
    local_sem, send_sem, recv_sem,
):
    dp = lax.axis_index("dp")
    ex = lax.axis_index("expert")
    z, x = dp // NX, dp % NX
    y, core = ex // 2, ex % 2
    zh, zl = z // 4, z % 4
    other = 1 - core

    @pl.when(core == 0)
    def _():
        pltpu.make_async_copy(tok_hbm, src, local_sem.at[0]).start()

    @pl.when(core == 1)
    def _():
        pltpu.make_async_copy(og_hbm, src, local_sem.at[0]).start()

    load_in = pltpu.make_async_copy(win_hbm.at[0], win, local_sem.at[1])
    load_out = pltpu.make_async_copy(wout_hbm.at[0], wout, local_sem.at[2])
    load_in.start()
    load_out.start()

    def mod4(v):
        return lax.rem(v + 4, 4)

    def mod16(v):
        return lax.rem(v + 16, 16)

    flip = 2 - 4 * (z % 2)
    near_z = [mod16(z + 1), mod16(z - 1), mod16(z + flip)]
    far_z = [mod4(zh + k) * 4 + zl for k in (1, -1, 2)]
    side_x = [mod4(x + k) for k in (1, -1, 2)]
    sibling = device(z, x, y, other)

    def pick(first, second):
        return first * other + second * core

    def near_dev(k):
        return device(near_z[k], x, y, core)

    stride_devs = [device(far_z[k], x, y, core) for k in range(3)]
    mid_devs = [device(pick(near_z[k], z), pick(x, side_x[k]), y, core) for k in range(3)]
    last_devs = [device(pick(z, near_z[k]), pick(side_x[k], x), y, core) for k in range(3)]
    y_devs = [device(z, x, lax.rem(y + k, NY), core) for k in range(1, NY)]
    i3 = pick(x, zl)
    i2 = pick(zl, x)
    tgt = (1, -1, 2)
    frm = (-1, 1, 2)

    barrier = pltpu.get_barrier_semaphore()
    greet = (
        stride_devs
        + [near_dev(0), near_dev(1), near_dev(2), device(mod16(z - flip), x, y, core)]
        + [device(z, side_x[k], y, core) for k in range(3)]
        + [sibling]
        + y_devs
    )
    for who in greet:
        pl.semaphore_signal(barrier, inc=1, device_id=who, device_id_type=MESH)

    counter = [0]

    def remote(src_ref, dst_ref, who):
        i = counter[0]
        counter[0] += 1
        return pltpu.make_async_remote_copy(
            src_ref=src_ref, dst_ref=dst_ref, send_sem=send_sem.at[i], recv_sem=recv_sem.at[i],
            device_id=who, device_id_type=MESH,
        )

    sent = []

    def go(copy):
        copy.start()
        sent.append(copy)
        return copy

    r48 = iota((48, 128), 0)
    slot48 = r48 >> 4
    p0, p1, p2 = picks[y, 0], picks[y, 1], picks[y, 2]
    pick48 = jnp.where(slot48 == 0, p0, jnp.where(slot48 == 1, p1, p2))
    hit48 = iota((48, 128), 1) == pick48
    chunk48 = r48 & 15
    pltpu.make_async_copy(tok_hbm, src, local_sem.at[0]).wait()
    own = jnp.zeros((48, 256), f32)
    for q in range(16):
        one = jnp.where(hit48 & (chunk48 == q), 1.0, 0.0).astype(bf16)
        own += jnp.dot(one, src[:, q * 256 : (q + 1) * 256], preferred_element_type=f32)
    rows_buf[core, i3, i2, zh] = own.astype(bf16)

    place = x * 16 + zl * 4 + zh
    spot = iota((8, 128), 0) * 128 + iota((8, 128), 1)
    mine = jnp.zeros((8, 128), f32)
    for j in range(SLOTS):
        wj = jnp.where(j < counts[y, 0], gates[y, j], 0.0)
        mine += jnp.where(spot == j * 64 + place, wj, 0.0)
    wt_own[0] = mine

    pl.semaphore_wait(barrier, len(greet))

    def exchange(views, devs, step):
        copies = []
        for k in range(3):
            copies.append(go(remote(views, views, devs[k])))
        small = []
        for k in range(3):
            small.append(go(remote(wt_own.at[step], wt_in.at[step, k], devs[k])))
        return copies, small

    def add_weights(step, small):
        for c in small:
            c.wait_recv()
        wt_own[step + 1] = wt_own[step] + ((wt_in[step, 0] + wt_in[step, 1]) + wt_in[step, 2])

    copies, small = exchange(rows_buf.at[core, i3, i2, zh], stride_devs, 0)
    add_weights(0, small)
    for c in copies:
        c.wait_recv()
    copies, small = exchange(rows_buf.at[core, i3, i2], mid_devs, 1)
    add_weights(1, small)
    for c in copies:
        c.wait_recv()
    copies, small = exchange(rows_buf.at[core, i3], last_devs, 2)
    hand = [go(remote(rows_buf.at[core, i3], rows_buf.at[core, i3], sibling))]
    add_weights(2, small)
    for k in range(3):
        copies[k].wait_recv()
        got = rows_buf.at[core, mod4(i3 + frm[k])]
        hand.append(go(remote(got, got, sibling)))
    for c in hand:
        c.wait_recv()

    qr, qc = iota((256, 256), 0), iota((256, 256), 1)
    turn = jnp.where(((qr >> 4) == (qc & 15)) & ((qr & 15) == (qc >> 4)), 1.0, 0.0).astype(bf16)

    def unfold(g, carry):
        for j in range(SLOTS):
            rows = pl.ds(pl.multiple_of(j * 64 + g * 16, 16), 16)
            tok16 = rows_buf[0, g, :, :, j * 16 : (j + 1) * 16, :].reshape(256, 256)
            og16 = rows_buf[1, :, g, :, j * 16 : (j + 1) * 16, :].reshape(256, 256)
            tok16 = jnp.dot(turn, tok16, preferred_element_type=f32).astype(bf16)
            og16 = jnp.dot(turn, og16, preferred_element_type=f32).astype(bf16)
            for q in range(16):
                full_tok[rows, q * 256 : (q + 1) * 256] = tok16[q * 16 : (q + 1) * 16]
                full_og[rows, q * 256 : (q + 1) * 256] = og16[q * 16 : (q + 1) * 16]
        return carry

    lax.fori_loop(0, 4, unfold, 0)

    load_in.wait()
    load_out.wait()
    contract_last = (((1,), (1,)), ((), ()))
    pre = lax.dot_general(win[...], full_tok[...], contract_last, preferred_element_type=f32)
    back = lax.dot_general(wout[...], full_og[...], contract_last, preferred_element_type=f32)
    wrow = jnp.concatenate([wt_own[3, 0:1, :], wt_own[3, 1:2, 0:64]], axis=1)
    inner = jnp.tanh(gelu_coef * (pre + cubic_coef * pre * pre * pre))
    act = 0.5 * pre * (1.0 + inner)
    slope = 0.5 * (1.0 + inner) + 0.5 * pre * (1.0 - inner * inner) * gelu_coef * (
        1.0 + 3.0 * cubic_coef * pre * pre
    )
    d_pre = back * wrow * slope
    d_low = d_pre.astype(bf16)
    act_low = (act * wrow).astype(bf16)
    srow = jnp.sum(act.astype(bf16).astype(f32) * back, axis=0, keepdims=True)
    scores = jnp.concatenate(
        [srow[:, 0:128], jnp.concatenate([srow[:, 128:192], jnp.zeros((1, 64), f32)], axis=1)], axis=0
    )
    score_own[0] = jnp.concatenate([scores, jnp.zeros((6, 128), f32)], axis=0)
    d_turn = jnp.transpose(d_pre).astype(bf16)

    def part(half, i):
        cols = pl.ds(pl.multiple_of((2 * i + half) * 256, 256), 256)
        return jnp.dot(d_turn, win[:, cols], preferred_element_type=f32)

    for i in range(8):
        part_send[:, i * 256 : (i + 1) * 256] = part(other, i).astype(bf16)
    swap = go(remote(part_send, part_in, sibling))
    swap_score = go(remote(score_own.at[0], score_in.at[0, 0], sibling))
    for i in range(8):
        part_own[:, i * 256 : (i + 1) * 256] = part(core, i)
    swap.wait_recv()

    for pair in range(2):
        for j in range(SLOTS):
            cols = []
            for g in (2 * pair, 2 * pair + 1):
                lo = j * 64 + g * 16
                both = part_own[lo : lo + 16, :] + part_in[lo : lo + 16, :].astype(f32)
                both = both.astype(bf16)
                cols.append(jnp.concatenate([both[:, q * 128 : (q + 1) * 128] for q in range(16)], axis=0))
            out = jnp.dot(turn, jnp.concatenate(cols, axis=1), preferred_element_type=f32).astype(bf16)
            for n in range(2):
                g = 2 * pair + n
                for d in range(4):
                    for h in range(4):
                        b = d * 4 + h
                        fold[pick(g, d), pick(d, g), h, j * 16 : (j + 1) * 16, :] = out[
                            b * 16 : (b + 1) * 16, n * 128 : (n + 1) * 128
                        ]

    def scatter(views, slots, devs, step):
        copies = [go(remote(views[k], slots.at[k], devs[k])) for k in range(3)]
        small = [go(remote(score_own.at[step], score_in.at[step, k], devs[k])) for k in range(3)]
        return copies, small

    def add_scores(step, small):
        for c in small:
            c.wait_recv()
        score_own[step + 1] = score_own[step] + (
            (score_in[step, 0] + score_in[step, 1]) + score_in[step, 2]
        )

    swap_score.wait_recv()
    score_own[1] = score_own[0] + score_in[0, 0]
    copies, small = scatter([fold.at[mod4(i3 + t)] for t in tgt], red1, last_devs, 1)

    def outer(i, carry):
        cols = pl.ds(pl.multiple_of(i * 512, 512), 512)
        gin[:, cols] = jnp.dot(d_low, full_tok[:, cols], preferred_element_type=f32).astype(bf16)
        gout[:, cols] = jnp.dot(act_low, full_og[:, cols], preferred_element_type=f32).astype(bf16)
        return carry

    lax.fori_loop(0, 8, outer, 0)
    store_in = pltpu.make_async_copy(gin, gin_hbm.at[0], local_sem.at[3])
    store_out = pltpu.make_async_copy(gout, gout_hbm.at[0], local_sem.at[4])
    store_in.start()
    store_out.start()

    add_scores(1, small)
    for c in copies:
        c.wait_recv()

    def sum_one(d, carry):
        t = (fold[i3, d].astype(f32) + red1[0, d].astype(f32)) + (
            red1[1, d].astype(f32) + red1[2, d].astype(f32)
        )
        sum1[d] = t.astype(bf16)
        return carry

    lax.fori_loop(0, 4, sum_one, 0)
    copies, small = scatter([sum1.at[mod4(i2 + t)] for t in tgt], red2, mid_devs, 2)
    add_scores(2, small)
    for c in copies:
        c.wait_recv()
    t = (sum1[i2].astype(f32) + red2[0].astype(f32)) + (red2[1].astype(f32) + red2[2].astype(f32))
    sum2[...] = t.astype(bf16)
    copies, small = scatter([sum2.at[mod4(zh + t)] for t in tgt], red3, stride_devs, 3)
    add_scores(3, small)
    for c in copies:
        c.wait_recv()
    total[...] = (sum2[zh].astype(f32) + red3[0].astype(f32)) + (
        red3[1].astype(f32) + red3[2].astype(f32)
    )

    final = score_own[4]
    r8, l8 = iota((8, 128), 0), iota((8, 128), 1)
    score_row = jnp.zeros((8, 128), f32)
    for j in range(SLOTS):
        s = jnp.sum(jnp.where(spot == j * 64 + place, final, 0.0), keepdims=True)
        score_row += jnp.where((r8 == 6) & (l8 == j), s, 0.0)
    for i in range(8):
        msg[i] = score_row
        for j in range(SLOTS):
            msg[i, 2 * j : 2 * j + 2, :] = total[16 * j + 2 * i : 16 * j + 2 * i + 2, :]
    last = [
        go(remote(msg.at[lax.rem(y + k, NY)], msg_in.at[y], y_devs[k - 1])) for k in range(1, NY)
    ]
    msg_in[y] = msg[y]
    for c in last:
        c.wait_recv()

    token = iota((128, 128), 0)
    for h in range(2):
        acc = jnp.zeros((128, 128), f32)
        for e in range(8):
            for j in range(SLOTS):
                acc += jnp.where(token == picks[e, j], msg_in[e, 2 * j + h : 2 * j + h + 1, :], 0.0)
        gtok_out[:, h * 128 : (h + 1) * 128] = acc.astype(bf16)
    for e in range(8):
        row = msg_in[e, 6:7, :]
        ggate_out[e : e + 1, :] = jnp.where(iota((1, 128), 1) < counts[e, 0], row, 0.0)

    for c in sent:
        c.wait_send()
    store_in.wait()
    store_out.wait()


def on_device(tokens, out_grad, w_in, w_out, gates, picks, counts):
    hbm = pl.BlockSpec(memory_space=pl.ANY)
    vmem = pl.BlockSpec(memory_space=pltpu.VMEM)
    smem = pl.BlockSpec(memory_space=pltpu.SMEM)
    sems = pltpu.SemaphoreType.DMA
    g_tok, g_in, g_out, g_gate = pl.pallas_call(
        kernel,
        out_shape=(
            jax.ShapeDtypeStruct((128, 256), bf16),
            jax.ShapeDtypeStruct((1, HID, D), bf16),
            jax.ShapeDtypeStruct((1, HID, D), bf16),
            jax.ShapeDtypeStruct((8, 128), f32),
        ),
        in_specs=[hbm, hbm, hbm, hbm, smem, smem, smem],
        out_specs=(vmem, hbm, hbm, vmem),
        scratch_shapes=[
            pltpu.VMEM((128, D), bf16),
            pltpu.VMEM((HID, D), bf16),
            pltpu.VMEM((HID, D), bf16),
            pltpu.VMEM((2, 4, 4, 4, 48, 256), bf16),
            pltpu.VMEM((192, D), bf16),
            pltpu.VMEM((192, D), bf16),
            pltpu.VMEM((4, 8, 128), f32),
            pltpu.VMEM((3, 3, 8, 128), f32),
            pltpu.VMEM((192, D // 2), f32),
            pltpu.VMEM((192, D // 2), bf16),
            pltpu.VMEM((192, D // 2), bf16),
            pltpu.VMEM((4, 4, 4, 48, 128), bf16),
            pltpu.VMEM((3, 4, 4, 48, 128), bf16),
            pltpu.VMEM((4, 4, 48, 128), bf16),
            pltpu.VMEM((3, 4, 48, 128), bf16),
            pltpu.VMEM((4, 48, 128), bf16),
            pltpu.VMEM((3, 48, 128), bf16),
            pltpu.VMEM((48, 128), f32),
            pltpu.VMEM((5, 8, 128), f32),
            pltpu.VMEM((4, 3, 8, 128), f32),
            pltpu.VMEM((8, 8, 128), f32),
            pltpu.VMEM((8, 8, 128), f32),
            pltpu.VMEM((HID, D), bf16),
            pltpu.VMEM((HID, D), bf16),
            sems((5,)),
            sems((56,)),
            sems((56,)),
        ],
        compiler_params=pltpu.CompilerParams(
            collective_id=0, has_side_effects=True, vmem_limit_bytes=48 * 2**20
        ),
        cost_estimate=pl.CostEstimate(flops=10**9, bytes_accessed=8 * 10**6, transcendentals=20000),
        name="expert_backward",
    )(tokens, out_grad, w_in, w_out, gates, picks, counts)
    return g_tok, g_in, g_out, g_gate[:, :SLOTS]


def solution(mesh):
    placed = (
        P("dp", None),
        P("dp", None),
        P("expert", "dp", None),
        P("expert", "dp", None),
        P(None, "dp"),
        P(None, "dp"),
        P(None, "dp"),
    )
    return jax.shard_map(
        on_device,
        mesh=mesh,
        in_specs=placed,
        out_specs=(
            P("dp", "expert"),
            P("expert", "dp", None),
            P("expert", "dp", None),
            P(None, "dp"),
        ),
        check_vma=False,
    )
```

time: 751 us -> 96.7 us (0.13)
  the two profiles are of different devices: /device:TPU:1 before, /device:TPU:64 now
where the time goes in v1:
time: 96.7 us; the launch traced here: 96.4 us
  Pallas kernels  86.4 us (89%)
  local copies, waits for them, and re-layouts  9.34 us (10%)
    pallas_call x1, Pallas kernels, on_device(): pl.pallas_call(kernel, out_shape=(jax.ShapeDtypeStruct((128, 256), bf16),...  86.4 us
    unnamed x19, local copies, waits for them, and re-layouts  9.34 us

profile of v1, /device:TPU:64, one launch (start us, length us, event | category | flops | bytes accessed | tf_op | source)
XLA Modules:
  0.0 96.4 jit_solution(14153286255762135890)
XLA Ops:
  0.6 0.0 copy-start.4
  0.6 0.8 copy.11.gates
  1.4 0.0 copy-done.4
  1.4 0.0 copy-start.5
  1.4 0.1 copy.12.picks
  1.5 0.6 copy-done.5
  2.1 0.1 copy.13.counts
  2.1 0.0 copy-start
  2.1 1.2 %copy-done = bf16[128,4096]{1,0:T(8,128)(2,1)S(1)} copy-done((bf16[128,4096]{1,0:T(8,128)(2,1)S(1)}, bf16[128,4096]{1,0:T(8,128)(2,1)}, u32[]{:S(2)}) %copy-start) | copy-done | bytes 1048600
  3.4 0.0 copy-start.1
  3.4 1.2 %copy-done.1 = bf16[128,4096]{1,0:T(8,128)(2,1)S(1)} copy-done((bf16[128,4096]{1,0:T(8,128)(2,1)S(1)}, bf16[128,4096]{1,0:T(8,128)(2,1)}, u32[]{:S(2)}) %copy-start.1) | copy-done | bytes 1048600
  4.6 0.0 copy-start.2
  4.6 1.2 %copy-done.2 = bf16[1,104,4096]{2,1,0:T(8,128)(2,1)S(1)} copy-done((bf16[1,104,4096]{2,1,0:T(8,128)(2,1)S(1)}, bf16[1,104,4096]{2,1,0:T(8,128)(2,1)}, u32[]{:S(2)}) %copy-start.2) | copy-done | bytes 851992
  5.8 0.0 copy-start.3
  5.8 1.2 %copy-done.3 = bf16[1,104,4096]{2,1,0:T(8,128)(2,1)S(1)} copy-done((bf16[1,104,4096]{2,1,0:T(8,128)(2,1)S(1)}, bf16[1,104,4096]{2,1,0:T(8,128)(2,1)}, u32[]{:S(2)}) %copy-start.3) | copy-done | bytes 851992
  6.9 86.4 %expert_backward.1 = (bf16[128,256]{1,0:T(8,128)(2,1)S(1)}, bf16[1,104,4096]{2,1,0:T(8,128)(2,1)S(1)}, bf16[1,104,4096]{2,1,0:T(8,128)(2,1)S(1)}, f32[8,128]{1,0:T(8,128)S(1)}) custom-call(bf16[128,4096]{1,0:T(8,128)(2,1)S(1)} %copy-done, bf16[128,4096]{1,0:T(8,128)(2,1)S(1)} %copy-done.1, bf16[1,104,4096]{2,1,0:T(8,128)(2,1)S(1)} %copy-done.2, ...), custom_call_target="tpu_custom_call" | custom-call | flops 1000000000 | bytes 8000000 | tf_op jit(solution)/shard_map/expert_backward/pallas_call | solution.py:328
  93.3 0.7 copy.14
  94.0 0.6 copy.18
  94.6 0.9 copy.19
  95.5 0.9 copy.20
Async XLA Ops:
  0.6 0.8 copy-start.4
  1.4 0.7 copy-start.5
  2.1 1.2 %copy-start = (bf16[128,4096]{1,0:T(8,128)(2,1)S(1)}, bf16[128,4096]{1,0:T(8,128)(2,1)}, u32[]{:S(2)}) copy-start(bf16[128,4096]{1,0:T(8,128)(2,1)} %tok_hbm.1) | copy-start | bytes 3145732
  3.4 1.2 %copy-start.1 = (bf16[128,4096]{1,0:T(8,128)(2,1)S(1)}, bf16[128,4096]{1,0:T(8,128)(2,1)}, u32[]{:S(2)}) copy-start(bf16[128,4096]{1,0:T(8,128)(2,1)} %og_hbm.1) | copy-start | bytes 3145732
  4.6 1.2 %copy-start.2 = (bf16[1,104,4096]{2,1,0:T(8,128)(2,1)S(1)}, bf16[1,104,4096]{2,1,0:T(8,128)(2,1)}, u32[]{:S(2)}) copy-start(bf16[1,104,4096]{2,1,0:T(8,128)(2,1)} %win_hbm.1) | copy-start | bytes 2555908
  5.8 1.2 %copy-start.3 = (bf16[1,104,4096]{2,1,0:T(8,128)(2,1)S(1)}, bf16[1,104,4096]{2,1,0:T(8,128)(2,1)}, u32[]{:S(2)}) copy-start(bf16[1,104,4096]{2,1,0:T(8,128)(2,1)} %wout_hbm.1) | copy-start | bytes 2555908

commit v2 on v1

--- a/solution.py
+++ b/solution.py
@@ -28,9 +28,9 @@
 
 def kernel(
     tok_hbm, og_hbm, win_hbm, wout_hbm, gates, picks, counts,
-    gtok_out, gin_hbm, gout_hbm, ggate_out,
-    src, win, wout, rows_buf, full_tok, full_og, wt_own, wt_in,
-    part_own, part_send, part_in, fold, red1, sum1, red2, sum2, red3, total,
+    msg_out, gate_out, gin_hbm, gout_hbm,
+    src, win, wout, rows_buf, full_tok, full_og,
+    part_own, part_send, part_in, fold, red1, sum1, red2, sum2,
     score_own, score_in, msg, msg_in, gin, gout,
     local_sem, send_sem, recv_sem,
 ):
@@ -61,9 +61,9 @@
         return lax.rem(v + 16, 16)
 
     flip = 2 - 4 * (z % 2)
-    near_z = [mod16(z + 1), mod16(z - 1), mod16(z + flip)]
-    far_z = [mod4(zh + k) * 4 + zl for k in (1, -1, 2)]
-    side_x = [mod4(x + k) for k in (1, -1, 2)]
+    near_z = [mod16(z + flip), mod16(z + 1), mod16(z - 1)]
+    far_z = [mod4(zh + k) * 4 + zl for k in (2, 1, -1)]
+    side_x = [mod4(x + k) for k in (2, 1, -1)]
     sibling = device(z, x, y, other)
 
     def pick(first, second):
@@ -75,19 +75,24 @@
     stride_devs = [device(far_z[k], x, y, core) for k in range(3)]
     mid_devs = [device(pick(near_z[k], z), pick(x, side_x[k]), y, core) for k in range(3)]
     last_devs = [device(pick(z, near_z[k]), pick(side_x[k], x), y, core) for k in range(3)]
-    y_devs = [device(z, x, lax.rem(y + k, NY), core) for k in range(1, NY)]
+    near4 = (0, 1, -1, 2)
+    end_devs = [
+        [device(mod4(zh + k) * 4 + zl, x, lax.rem(y + m, NY), core) for m in range(NY)] for k in near4
+    ]
     i3 = pick(x, zl)
     i2 = pick(zl, x)
-    tgt = (1, -1, 2)
-    frm = (-1, 1, 2)
+    tgt = (2, 1, -1)
+    frm = (2, -1, 1)
 
     barrier = pltpu.get_barrier_semaphore()
     greet = (
-        stride_devs
+        end_devs[0][1:]
+        + end_devs[1]
+        + end_devs[2]
+        + end_devs[3]
         + [near_dev(0), near_dev(1), near_dev(2), device(mod16(z - flip), x, y, core)]
         + [device(z, side_x[k], y, core) for k in range(3)]
         + [sibling]
-        + y_devs
     )
     for who in greet:
         pl.semaphore_signal(barrier, inc=1, device_id=who, device_id_type=MESH)
@@ -111,56 +116,50 @@
 
     r48 = iota((48, 128), 0)
     slot48 = r48 >> 4
-    p0, p1, p2 = picks[y, 0], picks[y, 1], picks[y, 2]
+    p0, p1, p2 = picks[0, y], picks[1, y], picks[2, y]
     pick48 = jnp.where(slot48 == 0, p0, jnp.where(slot48 == 1, p1, p2))
     hit48 = iota((48, 128), 1) == pick48
     chunk48 = r48 & 15
     pltpu.make_async_copy(tok_hbm, src, local_sem.at[0]).wait()
-    own = jnp.zeros((48, 256), f32)
-    for q in range(16):
-        one = jnp.where(hit48 & (chunk48 == q), 1.0, 0.0).astype(bf16)
-        own += jnp.dot(one, src[:, q * 256 : (q + 1) * 256], preferred_element_type=f32)
-    rows_buf[core, i3, i2, zh] = own.astype(bf16)
+    ones = [jnp.where(hit48 & (chunk48 == q), 1.0, 0.0).astype(bf16) for q in range(16)]
+    tall = jnp.concatenate([src[:, q * 256 : (q + 1) * 256] for q in range(16)], axis=0)
+    own = jnp.dot(jnp.concatenate(ones, axis=1), tall, preferred_element_type=f32)
+    slot_col = iota((48, 1), 0) >> 4
+    scale = jnp.zeros((48, 1), f32)
+    for j in range(SLOTS):
+        wj = jnp.where(j < counts[0, y], gates[j, y], 0.0)
+        scale = jnp.where(slot_col == j, wj, scale)
+    scale = jnp.where(core == 1, scale, 1.0)
+    rows_buf[core, i3, i2, zh] = (own * scale).astype(bf16)
 
     place = x * 16 + zl * 4 + zh
     spot = iota((8, 128), 0) * 128 + iota((8, 128), 1)
-    mine = jnp.zeros((8, 128), f32)
-    for j in range(SLOTS):
-        wj = jnp.where(j < counts[y, 0], gates[y, j], 0.0)
-        mine += jnp.where(spot == j * 64 + place, wj, 0.0)
-    wt_own[0] = mine
 
     pl.semaphore_wait(barrier, len(greet))
 
-    def exchange(views, devs, step):
-        copies = []
-        for k in range(3):
-            copies.append(go(remote(views, views, devs[k])))
-        small = []
-        for k in range(3):
-            small.append(go(remote(wt_own.at[step], wt_in.at[step, k], devs[k])))
-        return copies, small
-
-    def add_weights(step, small):
-        for c in small:
-            c.wait_recv()
-        wt_own[step + 1] = wt_own[step] + ((wt_in[step, 0] + wt_in[step, 1]) + wt_in[step, 2])
-
-    copies, small = exchange(rows_buf.at[core, i3, i2, zh], stride_devs, 0)
-    add_weights(0, small)
+    def exchange(views, devs):
+        return [go(remote(views, views, devs[k])) for k in range(3)]
+
+    def to_sibling(view):
+        hand.append(go(remote(view, view, sibling)))
+
+    hand = []
+    copies = exchange(rows_buf.at[core, i3, i2, zh], stride_devs)
     for c in copies:
         c.wait_recv()
-    copies, small = exchange(rows_buf.at[core, i3, i2], mid_devs, 1)
-    add_weights(1, small)
-    for c in copies:
-        c.wait_recv()
-    copies, small = exchange(rows_buf.at[core, i3], last_devs, 2)
-    hand = [go(remote(rows_buf.at[core, i3], rows_buf.at[core, i3], sibling))]
-    add_weights(2, small)
-    for k in range(3):
+    groups = [i2] + [mod4(i2 + frm[k]) for k in (1, 2, 0)]
+    copies = exchange(rows_buf.at[core, i3, i2], mid_devs)
+    chunks = [exchange(rows_buf.at[core, i3, i2], last_devs)]
+    to_sibling(rows_buf.at[core, i3, i2])
+    for n, k in enumerate((1, 2, 0)):
         copies[k].wait_recv()
-        got = rows_buf.at[core, mod4(i3 + frm[k])]
-        hand.append(go(remote(got, got, sibling)))
+        view = rows_buf.at[core, i3, groups[n + 1]]
+        chunks.append(exchange(view, last_devs))
+        to_sibling(view)
+    for n in range(4):
+        for k in (1, 2, 0):
+            chunks[n][k].wait_recv()
+            to_sibling(rows_buf.at[core, mod4(i3 + frm[k]), groups[n]])
     for c in hand:
         c.wait_recv()
 
@@ -186,16 +185,15 @@
     contract_last = (((1,), (1,)), ((), ()))
     pre = lax.dot_general(win[...], full_tok[...], contract_last, preferred_element_type=f32)
     back = lax.dot_general(wout[...], full_og[...], contract_last, preferred_element_type=f32)
-    wrow = jnp.concatenate([wt_own[3, 0:1, :], wt_own[3, 1:2, 0:64]], axis=1)
     inner = jnp.tanh(gelu_coef * (pre + cubic_coef * pre * pre * pre))
     act = 0.5 * pre * (1.0 + inner)
     slope = 0.5 * (1.0 + inner) + 0.5 * pre * (1.0 - inner * inner) * gelu_coef * (
         1.0 + 3.0 * cubic_coef * pre * pre
     )
-    d_pre = back * wrow * slope
+    d_pre = back * slope
     d_low = d_pre.astype(bf16)
-    act_low = (act * wrow).astype(bf16)
-    srow = jnp.sum(act.astype(bf16).astype(f32) * back, axis=0, keepdims=True)
+    act_low = act.astype(bf16)
+    srow = jnp.sum(act_low.astype(f32) * back, axis=0, keepdims=True)
     scores = jnp.concatenate(
         [srow[:, 0:128], jnp.concatenate([srow[:, 128:192], jnp.zeros((1, 64), f32)], axis=1)], axis=0
     )
@@ -276,48 +274,67 @@
     add_scores(2, small)
     for c in copies:
         c.wait_recv()
-    t = (sum1[i2].astype(f32) + red2[0].astype(f32)) + (red2[1].astype(f32) + red2[2].astype(f32))
-    sum2[...] = t.astype(bf16)
-    copies, small = scatter([sum2.at[mod4(zh + t)] for t in tgt], red3, stride_devs, 3)
-    add_scores(3, small)
-    for c in copies:
-        c.wait_recv()
-    total[...] = (sum2[zh].astype(f32) + red3[0].astype(f32)) + (
-        red3[1].astype(f32) + red3[2].astype(f32)
-    )
-
-    final = score_own[4]
-    r8, l8 = iota((8, 128), 0), iota((8, 128), 1)
-    score_row = jnp.zeros((8, 128), f32)
-    for j in range(SLOTS):
-        s = jnp.sum(jnp.where(spot == j * 64 + place, final, 0.0), keepdims=True)
-        score_row += jnp.where((r8 == 6) & (l8 == j), s, 0.0)
-    for i in range(8):
-        msg[i] = score_row
-        for j in range(SLOTS):
-            msg[i, 2 * j : 2 * j + 2, :] = total[16 * j + 2 * i : 16 * j + 2 * i + 2, :]
-    last = [
-        go(remote(msg.at[lax.rem(y + k, NY)], msg_in.at[y], y_devs[k - 1])) for k in range(1, NY)
-    ]
-    msg_in[y] = msg[y]
+    sum2[...] = (sum1[i2].astype(f32) + red2[0].astype(f32)) + (
+        red2[1].astype(f32) + red2[2].astype(f32)
+    )
+
+    for h in range(4):
+        for i in range(NY):
+            for j in range(SLOTS):
+                msg[h, i, 2 * j : 2 * j + 2, :] = sum2[h, 16 * j + 2 * i : 16 * j + 2 * i + 2, :]
+            msg[h, i, 6:8, :] = score_own[3, 0:2, :]
+    last = []
+    for k in (3, 1, 2, 0):
+        to_h = mod4(zh + near4[k])
+        for m in (4, 3, 5, 2, 6, 1, 7, 0):
+            if k + m > 0:
+                to_y = lax.rem(y + m, NY)
+                last.append(go(remote(msg.at[to_h, to_y], msg_in.at[zh, y], end_devs[k][m])))
+    msg_in[zh, y] = msg[zh, y]
     for c in last:
         c.wait_recv()
-
+    got = (msg_in[0] + msg_in[1]) + (msg_in[2] + msg_in[3])
+    msg_out[...] = got
+    r8, l8 = iota((8, 128), 0), iota((8, 128), 1)
+    gate = jnp.zeros((8, 128), f32)
+    for j in range(SLOTS):
+        line = got[:, 6 + j // 2, :]
+        mine = jnp.sum(jnp.where(l8 == (j % 2) * 64 + place, line, 0.0), axis=1, keepdims=True)
+        flat = jnp.sum(jnp.where(l8 == r8, mine, 0.0), axis=0, keepdims=True)
+        gate += jnp.where(r8 == j, flat, 0.0)
+    gate_out[...] = gate
+
+    for c in sent:
+        c.wait_send()
+    store_in.wait()
+    store_out.wait()
+
+
+def finish(msg_in, gate, gin_in, gout_in, picks, counts, gates, gtok_out, gin_hbm, gout_hbm, ggate_out, stage, sem):
+    loads = [
+        pltpu.make_async_copy(gin_in.at[0], stage.at[0], sem.at[0]),
+        pltpu.make_async_copy(gout_in.at[0], stage.at[1], sem.at[1]),
+    ]
+    stores = [
+        pltpu.make_async_copy(stage.at[0], gin_hbm.at[0], sem.at[2]),
+        pltpu.make_async_copy(stage.at[1], gout_hbm.at[0], sem.at[3]),
+    ]
+    for c in loads:
+        c.start()
+    for load, store in zip(loads, stores):
+        load.wait()
+        store.start()
     token = iota((128, 128), 0)
     for h in range(2):
         acc = jnp.zeros((128, 128), f32)
         for e in range(8):
             for j in range(SLOTS):
-                acc += jnp.where(token == picks[e, j], msg_in[e, 2 * j + h : 2 * j + h + 1, :], 0.0)
+                acc += jnp.where(token == picks[j, e], msg_in[e, 2 * j + h : 2 * j + h + 1, :], 0.0)
         gtok_out[:, h * 128 : (h + 1) * 128] = acc.astype(bf16)
-    for e in range(8):
-        row = msg_in[e, 6:7, :]
-        ggate_out[e : e + 1, :] = jnp.where(iota((1, 128), 1) < counts[e, 0], row, 0.0)
-
-    for c in sent:
-        c.wait_send()
-    store_in.wait()
-    store_out.wait()
+    ok = iota((SLOTS, 8), 0) < counts[...]
+    ggate_out[...] = jnp.where(ok, gate[0:SLOTS, 0:8] / gates[...], 0.0)
+    for c in stores:
+        c.wait()
 
 
 def on_device(tokens, out_grad, w_in, w_out, gates, picks, counts):
@@ -325,16 +342,17 @@
     vmem = pl.BlockSpec(memory_space=pltpu.VMEM)
     smem = pl.BlockSpec(memory_space=pltpu.SMEM)
     sems = pltpu.SemaphoreType.DMA
-    g_tok, g_in, g_out, g_gate = pl.pallas_call(
+    gates, picks, counts = gates.T, picks.T, counts.T
+    received, gate, g_in, g_out = pl.pallas_call(
         kernel,
         out_shape=(
-            jax.ShapeDtypeStruct((128, 256), bf16),
+            jax.ShapeDtypeStruct((8, 8, 128), f32),
+            jax.ShapeDtypeStruct((8, 128), f32),
             jax.ShapeDtypeStruct((1, HID, D), bf16),
             jax.ShapeDtypeStruct((1, HID, D), bf16),
-            jax.ShapeDtypeStruct((8, 128), f32),
         ),
         in_specs=[hbm, hbm, hbm, hbm, smem, smem, smem],
-        out_specs=(vmem, hbm, hbm, vmem),
+        out_specs=(vmem, vmem, hbm, hbm),
         scratch_shapes=[
             pltpu.VMEM((128, D), bf16),
             pltpu.VMEM((HID, D), bf16),
@@ -342,8 +360,6 @@
             pltpu.VMEM((2, 4, 4, 4, 48, 256), bf16),
             pltpu.VMEM((192, D), bf16),
             pltpu.VMEM((192, D), bf16),
-            pltpu.VMEM((4, 8, 128), f32),
-            pltpu.VMEM((3, 3, 8, 128), f32),
             pltpu.VMEM((192, D // 2), f32),
             pltpu.VMEM((192, D // 2), bf16),
             pltpu.VMEM((192, D // 2), bf16),
@@ -351,26 +367,37 @@
             pltpu.VMEM((3, 4, 4, 48, 128), bf16),
             pltpu.VMEM((4, 4, 48, 128), bf16),
             pltpu.VMEM((3, 4, 48, 128), bf16),
-            pltpu.VMEM((4, 48, 128), bf16),
-            pltpu.VMEM((3, 48, 128), bf16),
-            pltpu.VMEM((48, 128), f32),
+            pltpu.VMEM((4, 48, 128), f32),
             pltpu.VMEM((5, 8, 128), f32),
             pltpu.VMEM((4, 3, 8, 128), f32),
-            pltpu.VMEM((8, 8, 128), f32),
-            pltpu.VMEM((8, 8, 128), f32),
+            pltpu.VMEM((4, NY, 8, 128), f32),
+            pltpu.VMEM((4, NY, 8, 128), f32),
             pltpu.VMEM((HID, D), bf16),
             pltpu.VMEM((HID, D), bf16),
             sems((5,)),
-            sems((56,)),
-            sems((56,)),
+            sems((96,)),
+            sems((96,)),
         ],
         compiler_params=pltpu.CompilerParams(
-            collective_id=0, has_side_effects=True, vmem_limit_bytes=48 * 2**20
+            collective_id=0, has_side_effects=True, vmem_limit_bytes=60 * 2**20
         ),
         cost_estimate=pl.CostEstimate(flops=10**9, bytes_accessed=8 * 10**6, transcendentals=20000),
         name="expert_backward",
     )(tokens, out_grad, w_in, w_out, gates, picks, counts)
-    return g_tok, g_in, g_out, g_gate[:, :SLOTS]
+    g_tok, g_in, g_out, g_gate = pl.pallas_call(
+        finish,
+        out_shape=(
+            jax.ShapeDtypeStruct((128, 256), bf16),
+            jax.ShapeDtypeStruct((1, HID, D), bf16),
+            jax.ShapeDtypeStruct((1, HID, D), bf16),
+            jax.ShapeDtypeStruct((SLOTS, 8), f32),
+        ),
+        in_specs=[vmem, vmem, hbm, hbm, smem, vmem, vmem],
+        out_specs=(vmem, hbm, hbm, vmem),
+        scratch_shapes=[pltpu.VMEM((2, HID, D), bf16), sems((4,))],
+        name="finish",
+    )(received, gate, g_in, g_out, picks, counts, gates)
+    return g_tok, g_in, g_out, g_gate.T
 
 
 def solution(mesh):

time: 96.7 us -> 84.8 us (0.88)
  local copies, waits for them, and re-layouts: 9.34 us -> 0 us
  Pallas kernels: 86.4 us -> 83.9 us
    unnamed x19 -> x0, local copies, waits for them, and re-layouts: 9.34 us -> none
    pallas_call x1 -> x2, Pallas kernels: 86.4 us -> 83.9 us  [the longest x1 80 us: on_device(): pl.pallas_call(kernel, out_shape=(jax.ShapeDtypeStruct((8, 8, 128), f32),...]
where the time goes in v2:
time: 84.8 us; the launch traced here: 84.5 us
  Pallas kernels  83.9 us (99%)
    pallas_call x1, Pallas kernels, on_device(): pl.pallas_call(kernel, out_shape=(jax.ShapeDtypeStruct((8, 8, 128), f32),...  80 us
    pallas_call x1, Pallas kernels, on_device(): pl.pallas_call(finish, out_shape=(jax.ShapeDtypeStruct((128, 256), bf16),...  3.83 us

profile of v2, /device:TPU:64, one launch (start us, length us, event | category | flops | bytes accessed | tf_op | source)
XLA Modules:
  0.0 84.5 jit_solution(14845843378656040090)
XLA Ops:
  0.6 80.0 %expert_backward.1 = (f32[8,8,128]{2,1,0:T(8,128)}, f32[8,128]{1,0:T(8,128)}, bf16[1,104,4096]{2,1,0:T(8,128)(2,1)}, bf16[1,104,4096]{2,1,0:T(8,128)(2,1)}) custom-call(bf16[128,4096]{1,0:T(8,128)(2,1)} %tok_hbm.1, bf16[128,4096]{1,0:T(8,128)(2,1)} %og_hbm.1, bf16[1,104,4096]{2,1,0:T(8,128)(2,1)} %win_hbm.1, bf16[1,104,4096]{2,1,0:T(8,128)(2,1)} %wout_hbm.1, ...), custom_call_target="tpu_custom_call" | custom-call | flops 1000000000 | bytes 8000000 | tf_op jit(solution)/shard_map/expert_backward/pallas_call | solution.py:346
  80.7 3.8 %finish.1 = (bf16[128,256]{1,0:T(8,128)(2,1)}, bf16[1,104,4096]{2,1,0:T(8,128)(2,1)}, bf16[1,104,4096]{2,1,0:T(8,128)(2,1)}, f32[3,8]{1,0:T(4,128)}) custom-call(f32[8,8,128]{2,1,0:T(8,128)} %get-tuple-element.12.msg_in, f32[8,128]{1,0:T(8,128)} %get-tuple-element.13.gate, bf16[1,104,4096]{2,1,0:T(8,128)(2,1)} %get-tuple-element.14.gin_in, ...), custom_call_target="tpu_custom_call" | custom-call | tf_op jit(solution)/shard_map/finish/pallas_call | solution.py:387

commit v3 on v2

--- a/solution.py
+++ b/solution.py
@@ -28,10 +28,10 @@
 
 def kernel(
     tok_hbm, og_hbm, win_hbm, wout_hbm, gates, picks, counts,
-    msg_out, gate_out, gin_hbm, gout_hbm,
+    gtok_out, gate_out, gin_hbm, gout_hbm,
     src, win, wout, rows_buf, full_tok, full_og,
-    part_own, part_send, part_in, fold, red1, sum1, red2, sum2,
-    score_own, score_in, msg, msg_in, gin, gout,
+    part_own, part_send, part_in, fold, red1, sum1, msg2, in2, sum2, msg3, in3,
+    score_own, score_in, gin, gout,
     local_sem, send_sem, recv_sem,
 ):
     dp = lax.axis_index("dp")
@@ -69,31 +69,20 @@
     def pick(first, second):
         return first * other + second * core
 
-    def near_dev(k):
-        return device(near_z[k], x, y, core)
-
     stride_devs = [device(far_z[k], x, y, core) for k in range(3)]
-    mid_devs = [device(pick(near_z[k], z), pick(x, side_x[k]), y, core) for k in range(3)]
+    from_z = [mod16(z - flip), mod16(z + 1), mod16(z - 1)]
+    mid_z, mid_x = [pick(near_z[k], z) for k in range(3)], [pick(x, side_x[k]) for k in range(3)]
+    mid_devs = [device(mid_z[k], mid_x[k], y, core) for k in range(3)]
     last_devs = [device(pick(z, near_z[k]), pick(side_x[k], x), y, core) for k in range(3)]
-    near4 = (0, 1, -1, 2)
-    end_devs = [
-        [device(mod4(zh + k) * 4 + zl, x, lax.rem(y + m, NY), core) for m in range(NY)] for k in near4
-    ]
     i3 = pick(x, zl)
     i2 = pick(zl, x)
     tgt = (2, 1, -1)
     frm = (2, -1, 1)
 
     barrier = pltpu.get_barrier_semaphore()
-    greet = (
-        end_devs[0][1:]
-        + end_devs[1]
-        + end_devs[2]
-        + end_devs[3]
-        + [near_dev(0), near_dev(1), near_dev(2), device(mod16(z - flip), x, y, core)]
-        + [device(z, side_x[k], y, core) for k in range(3)]
-        + [sibling]
-    )
+    greet = [device(pick(from_z[k], z), mid_x[k], lax.rem(y + m, NY), core) for m in range(NY) for k in range(3)]
+    greet += [device(pick(z, from_z[k]), pick(side_x[k], x), y, core) for k in range(3)]
+    greet += stride_devs + [device(z, x, lax.rem(y + m, NY), core) for m in range(1, NY)] + [sibling]
     for who in greet:
         pl.semaphore_signal(barrier, inc=1, device_id=who, device_id_type=MESH)
 
@@ -212,6 +201,7 @@
         part_own[:, i * 256 : (i + 1) * 256] = part(core, i)
     swap.wait_recv()
 
+    order = [2 * i + h for h in range(2) for i in range(NY)]
     for pair in range(2):
         for j in range(SLOTS):
             cols = []
@@ -219,7 +209,7 @@
                 lo = j * 64 + g * 16
                 both = part_own[lo : lo + 16, :] + part_in[lo : lo + 16, :].astype(f32)
                 both = both.astype(bf16)
-                cols.append(jnp.concatenate([both[:, q * 128 : (q + 1) * 128] for q in range(16)], axis=0))
+                cols.append(jnp.concatenate([both[:, q * 128 : (q + 1) * 128] for q in order], axis=0))
             out = jnp.dot(turn, jnp.concatenate(cols, axis=1), preferred_element_type=f32).astype(bf16)
             for n in range(2):
                 g = 2 * pair + n
@@ -266,35 +256,50 @@
         t = (fold[i3, d].astype(f32) + red1[0, d].astype(f32)) + (
             red1[1, d].astype(f32) + red1[2, d].astype(f32)
         )
-        sum1[d] = t.astype(bf16)
+        sum1[d] = t
         return carry
 
     lax.fori_loop(0, 4, sum_one, 0)
-    copies, small = scatter([sum1.at[mod4(i2 + t)] for t in tgt], red2, mid_devs, 2)
-    add_scores(2, small)
-    for c in copies:
+    def pack(d, carry):
+        lines = score_own[2, 0:2, :]
+        for i in range(NY):
+            parts = []
+            for h in range(4):
+                parts.append(sum1[d, h, pl.ds(i, 6, stride=8), :])
+                parts.append(lines)
+            msg2[d, i] = jnp.concatenate(parts, axis=0).astype(bf16)
+        return carry
+
+    lax.fori_loop(0, 4, pack, 0)
+    second = []
+    for m in (4, 3, 5, 2, 6, 1, 7, 0):
+        to_y = lax.rem(y + m, NY)
+        for k in range(4):
+            if k < 3:
+                who = device(mid_z[k], mid_x[k], to_y, core)
+                second.append(go(remote(msg2.at[mod4(i2 + tgt[k]), to_y], in2.at[k, y], who)))
+            elif m > 0:
+                who = device(z, x, to_y, core)
+                second.append(go(remote(msg2.at[i2, to_y], in2.at[3, y], who)))
+    in2[3, y] = msg2[i2, y]
+    for c in second:
         c.wait_recv()
-    sum2[...] = (sum1[i2].astype(f32) + red2[0].astype(f32)) + (
-        red2[1].astype(f32) + red2[2].astype(f32)
-    )
-
+    sum2[...] = (in2[0].astype(f32) + in2[1].astype(f32)) + (in2[2].astype(f32) + in2[3].astype(f32))
     for h in range(4):
-        for i in range(NY):
+        msg3[h] = sum2[:, h * 8 : (h + 1) * 8, :].reshape(64, 128).astype(bf16)
+    third = [go(remote(msg3.at[mod4(zh + tgt[k])], in3.at[k], stride_devs[k])) for k in range(3)]
+    got = sum2[:, pl.ds(pl.multiple_of(zh * 8, 8), 8), :]
+    for c in third:
+        c.wait_recv()
+    came = (in3[0].astype(f32) + in3[1].astype(f32)) + in3[2].astype(f32)
+    got = got + came.reshape(NY, 8, 128)
+    token = iota((128, 128), 0)
+    for h in range(2):
+        acc = jnp.zeros((128, 128), f32)
+        for e in range(8):
             for j in range(SLOTS):
-                msg[h, i, 2 * j : 2 * j + 2, :] = sum2[h, 16 * j + 2 * i : 16 * j + 2 * i + 2, :]
-            msg[h, i, 6:8, :] = score_own[3, 0:2, :]
-    last = []
-    for k in (3, 1, 2, 0):
-        to_h = mod4(zh + near4[k])
-        for m in (4, 3, 5, 2, 6, 1, 7, 0):
-            if k + m > 0:
-                to_y = lax.rem(y + m, NY)
-                last.append(go(remote(msg.at[to_h, to_y], msg_in.at[zh, y], end_devs[k][m])))
-    msg_in[zh, y] = msg[zh, y]
-    for c in last:
-        c.wait_recv()
-    got = (msg_in[0] + msg_in[1]) + (msg_in[2] + msg_in[3])
-    msg_out[...] = got
+                acc += jnp.where(token == picks[j, e], got[e, 2 * j + h : 2 * j + h + 1, :], 0.0)
+        gtok_out[:, h * 128 : (h + 1) * 128] = acc.astype(bf16)
     r8, l8 = iota((8, 128), 0), iota((8, 128), 1)
     gate = jnp.zeros((8, 128), f32)
     for j in range(SLOTS):
@@ -302,7 +307,12 @@
         mine = jnp.sum(jnp.where(l8 == (j % 2) * 64 + place, line, 0.0), axis=1, keepdims=True)
         flat = jnp.sum(jnp.where(l8 == r8, mine, 0.0), axis=0, keepdims=True)
         gate += jnp.where(r8 == j, flat, 0.0)
-    gate_out[...] = gate
+    held, full = jnp.ones((8, 128), f32), jnp.zeros((8, 128), jnp.int32)
+    for e in range(8):
+        full = jnp.where(l8 == e, counts[0, e], full)
+        for j in range(SLOTS):
+            held = jnp.where((r8 == j) & (l8 == e), gates[j, e], held)
+    gate_out[...] = jnp.where(r8 < full, gate / held, 0.0)
 
     for c in sent:
         c.wait_send()
@@ -310,29 +320,15 @@
     store_out.wait()
 
 
-def finish(msg_in, gate, gin_in, gout_in, picks, counts, gates, gtok_out, gin_hbm, gout_hbm, ggate_out, stage, sem):
-    loads = [
-        pltpu.make_async_copy(gin_in.at[0], stage.at[0], sem.at[0]),
-        pltpu.make_async_copy(gout_in.at[0], stage.at[1], sem.at[1]),
+def finish(gtok_in, gate, gin_in, gout_in, gtok_hbm, gin_hbm, gout_hbm, ggate_out, sem):
+    stores = [
+        pltpu.make_async_copy(gin_in, gin_hbm, sem.at[0]),
+        pltpu.make_async_copy(gout_in, gout_hbm, sem.at[1]),
+        pltpu.make_async_copy(gtok_in, gtok_hbm, sem.at[2]),
     ]
-    stores = [
-        pltpu.make_async_copy(stage.at[0], gin_hbm.at[0], sem.at[2]),
-        pltpu.make_async_copy(stage.at[1], gout_hbm.at[0], sem.at[3]),
-    ]
-    for c in loads:
+    for c in stores:
         c.start()
-    for load, store in zip(loads, stores):
-        load.wait()
-        store.start()
-    token = iota((128, 128), 0)
-    for h in range(2):
-        acc = jnp.zeros((128, 128), f32)
-        for e in range(8):
-            for j in range(SLOTS):
-                acc += jnp.where(token == picks[j, e], msg_in[e, 2 * j + h : 2 * j + h + 1, :], 0.0)
-        gtok_out[:, h * 128 : (h + 1) * 128] = acc.astype(bf16)
-    ok = iota((SLOTS, 8), 0) < counts[...]
-    ggate_out[...] = jnp.where(ok, gate[0:SLOTS, 0:8] / gates[...], 0.0)
+    ggate_out[...] = gate[0:SLOTS, 0:8]
     for c in stores:
         c.wait()
 
@@ -343,13 +339,13 @@
     smem = pl.BlockSpec(memory_space=pltpu.SMEM)
     sems = pltpu.SemaphoreType.DMA
     gates, picks, counts = gates.T, picks.T, counts.T
-    received, gate, g_in, g_out = pl.pallas_call(
+    g_tok, gate, g_in, g_out = pl.pallas_call(
         kernel,
         out_shape=(
-            jax.ShapeDtypeStruct((8, 8, 128), f32),
-            jax.ShapeDtypeStruct((8, 128), f32),
-            jax.ShapeDtypeStruct((1, HID, D), bf16),
-            jax.ShapeDtypeStruct((1, HID, D), bf16),
+            pltpu.VMEM((128, 256), bf16),
+            pltpu.VMEM((8, 128), f32),
+            pltpu.VMEM((1, HID, D), bf16),
+            pltpu.VMEM((1, HID, D), bf16),
         ),
         in_specs=[hbm, hbm, hbm, hbm, smem, smem, smem],
         out_specs=(vmem, vmem, hbm, hbm),
@@ -365,13 +361,14 @@
             pltpu.VMEM((192, D // 2), bf16),
             pltpu.VMEM((4, 4, 4, 48, 128), bf16),
             pltpu.VMEM((3, 4, 4, 48, 128), bf16),
-            pltpu.VMEM((4, 4, 48, 128), bf16),
-            pltpu.VMEM((3, 4, 48, 128), bf16),
-            pltpu.VMEM((4, 48, 128), f32),
+            pltpu.VMEM((4, 4, 48, 128), f32),
+            pltpu.VMEM((4, NY, 32, 128), bf16),
+            pltpu.VMEM((4, NY, 32, 128), bf16),
+            pltpu.VMEM((NY, 32, 128), f32),
+            pltpu.VMEM((4, 64, 128), bf16),
+            pltpu.VMEM((3, 64, 128), bf16),
             pltpu.VMEM((5, 8, 128), f32),
             pltpu.VMEM((4, 3, 8, 128), f32),
-            pltpu.VMEM((4, NY, 8, 128), f32),
-            pltpu.VMEM((4, NY, 8, 128), f32),
             pltpu.VMEM((HID, D), bf16),
             pltpu.VMEM((HID, D), bf16),
             sems((5,)),
@@ -379,7 +376,7 @@
             sems((96,)),
         ],
         compiler_params=pltpu.CompilerParams(
-            collective_id=0, has_side_effects=True, vmem_limit_bytes=60 * 2**20
+            collective_id=0, has_side_effects=True, vmem_limit_bytes=58 * 2**20
         ),
         cost_estimate=pl.CostEstimate(flops=10**9, bytes_accessed=8 * 10**6, transcendentals=20000),
         name="expert_backward",
@@ -392,11 +389,12 @@
             jax.ShapeDtypeStruct((1, HID, D), bf16),
             jax.ShapeDtypeStruct((SLOTS, 8), f32),
         ),
-        in_specs=[vmem, vmem, hbm, hbm, smem, vmem, vmem],
-        out_specs=(vmem, hbm, hbm, vmem),
-        scratch_shapes=[pltpu.VMEM((2, HID, D), bf16), sems((4,))],
+        in_specs=[hbm, vmem, hbm, hbm],
+        out_specs=(hbm, hbm, hbm, vmem),
+        scratch_shapes=[sems((3,))],
+        compiler_params=pltpu.CompilerParams(vmem_limit_bytes=6 * 2**20),
         name="finish",
-    )(received, gate, g_in, g_out, picks, counts, gates)
+    )(g_tok, gate, g_in, g_out)
     return g_tok, g_in, g_out, g_gate.T
 
 

time: 84.8 us -> 81.7 us (0.963)
  the two profiles are of different devices: /device:TPU:64 before, /device:TPU:17 now
where the time goes in v3:
time: 81.7 us; the launch traced here: 81.5 us
  Pallas kernels  80.9 us (99%)
    pallas_call x1, Pallas kernels, on_device(): pl.pallas_call(kernel, out_shape=(pltpu.VMEM((128, 256), bf16), pltpu.VME...  79.1 us
    pallas_call x1, Pallas kernels, on_device(): pl.pallas_call(finish, out_shape=(jax.ShapeDtypeStruct((128, 256), bf16),...  1.8 us

profile of v3, /device:TPU:17, one launch (start us, length us, event | category | flops | bytes accessed | tf_op | source)
XLA Modules:
  0.0 81.5 jit_solution(753467361351852366)
XLA Ops:
  0.6 79.1 %expert_backward.1 = (bf16[128,256]{1,0:T(8,128)(2,1)S(1)}, f32[8,128]{1,0:T(8,128)S(1)}, bf16[1,104,4096]{2,1,0:T(8,128)(2,1)S(1)}, bf16[1,104,4096]{2,1,0:T(8,128)(2,1)S(1)}) custom-call(bf16[128,4096]{1,0:T(8,128)(2,1)} %tok_hbm.1, bf16[128,4096]{1,0:T(8,128)(2,1)} %og_hbm.1, bf16[1,104,4096]{2,1,0:T(8,128)(2,1)} %win_hbm.1, ...), custom_call_target="tpu_custom_call" | custom-call | flops 1000000000 | bytes 8000000 | tf_op jit(solution)/shard_map/expert_backward/pallas_call | solution.py:342
  79.7 1.8 %finish.1 = (bf16[128,256]{1,0:T(8,128)(2,1)}, bf16[1,104,4096]{2,1,0:T(8,128)(2,1)}, bf16[1,104,4096]{2,1,0:T(8,128)(2,1)}, f32[3,8]{1,0:T(4,128)}) custom-call(bf16[128,256]{1,0:T(8,128)(2,1)S(1)} %get-tuple-element.12.gtok_in, f32[8,128]{1,0:T(8,128)S(1)} %get-tuple-element.13.gate, bf16[1,104,4096]{2,1,0:T(8,128)(2,1)S(1)} %get-tuple-element.14.gin_in, ...), custom_call_target="tpu_custom_call" | custom-call | tf_op jit(solution)/shard_map/finish/pallas_call | solution.py:384
